TPU v7x, 32 devices: a whole 2x2x4 slice. The times are simulated.
32 devices in a mesh: groups: 2 (over x), dp: 8 (over z, y), tensor: 2 (over core).
Axes of the slice: x: 2, y: 2, z: 4, core: 2. Of those that a mesh axis runs over, the one named last changes fastest.
Arguments:
- x_in: bfloat16 [1536, 8192], P(('groups', 'dp'), 'tensor'), parts along dimension 0, may hold values from -6 to 6
- gate_pre: bfloat16 [1536, 28672], P(('groups', 'dp'), 'tensor'), parts along dimension 0, may hold values from -6 to 6
- up_pre: bfloat16 [1536, 28672], P(('groups', 'dp'), 'tensor'), parts along dimension 0, may hold values from -6 to 6
- grad_hidden: bfloat16 [1536, 28672], P(('groups', 'dp'), 'tensor'), parts along dimension 0, may hold values from -6 to 6
- grad_out: bfloat16 [1536, 8192], P(('groups', 'dp'), 'tensor'), parts along dimension 0, may hold values from -6 to 6
- proj_model: bfloat16 [64, 8192], P('dp', 'tensor'), may hold values from -0.0625 to 0.0625
- proj_hidden: bfloat16 [64, 28672], P('dp', 'tensor'), may hold values from -0.03125 to 0.03125
- lengths: int32 [8], P('groups'), parts along dimension 0, may hold values from 1 to 384, 768 in all
- queries: bfloat16 [512, 12288], P(('groups', 'dp'), 'tensor'), parts along dimension 0, may hold values from -0.0546875 to 0.0546875
- cand: int32 [8, 8], P('groups'), parts along dimension 0, may hold values from 0 to 7
- cand_count: int32 [8], P('groups'), parts along dimension 0, may hold values from 1 to 8
Outputs:
- scores: float32 [8, 8, 32], P('groups'), parts along dimension 0
There are 2 independent parts, one for each index of `groups`. A program takes and returns all parts, laid end to end along the dimension named above; an argument that names none is the same for every part. Nothing has to cross between parts.
Inputs may be any that keep to these rules, and one draw needn't show every extreme that they name: The lengths sum to 768; sequence s occupies the tokens that follow those of sequences 0 to s - 1.
All inputs are finite; a program needn't handle non-finite values.
Results may differ from a plain program's by a relative error of at most 0.0042.
Values may be sent and summed in bfloat16 or wider, within the bound.
A program may use at most 64 MiB of HBM per device.

v0:
```python
import jax
import jax.numpy as jnp
from jax import lax
from jax.sharding import PartitionSpec as P

QBS = 32
CAND = 8


def contract_rows(left, right):
    return lax.dot_general(
        left, right, (((1,), (1,)), ((), ())), preferred_element_type=jnp.float32
    )


def local(
    x_in,
    gate_pre,
    up_pre,
    grad_hidden,
    grad_out,
    proj_model,
    proj_hidden,
    lengths,
    queries,
    cand,
    cand_count,
):
    model_rows, hidden_rows = (
        lax.all_gather(proj_model, "dp", axis=0, tiled=True),
        lax.all_gather(proj_hidden, "dp", axis=0, tiled=True),
    )
    gate_f = gate_pre.astype(jnp.float32)
    up_f = up_pre.astype(jnp.float32)
    grad_f = grad_hidden.astype(jnp.float32)
    sig_gate = jax.nn.sigmoid(gate_f)
    hidden_act = (gate_f * sig_gate * up_f).astype(jnp.bfloat16)
    grad_gate = (grad_f * up_f * sig_gate * (1.0 + gate_f * (1.0 - sig_gate))).astype(jnp.bfloat16)
    grad_up = (grad_f * gate_f * sig_gate).astype(jnp.bfloat16)
    partial_proj = jnp.concatenate(
        [
            contract_rows(x_in, model_rows),
            contract_rows(hidden_act, hidden_rows),
            contract_rows(grad_gate, hidden_rows),
            contract_rows(grad_up, hidden_rows),
            contract_rows(grad_out, model_rows),
        ],
        axis=1,
    )
    summed = lax.psum(partial_proj, "tensor")
    rank_size = model_rows.shape[0]
    half_rank = rank_size // lax.axis_size("tensor")
    core_index = lax.axis_index("tensor")
    model_proj = summed[:, 0:rank_size]
    hidden_proj = summed[:, rank_size : 2 * rank_size]
    gate_proj = summed[:, 2 * rank_size : 3 * rank_size]
    up_proj = summed[:, 3 * rank_size : 4 * rank_size]
    out_proj = summed[:, 4 * rank_size : 5 * rank_size]
    seq_count = lengths.shape[0]
    tok_count = x_in.shape[0]
    position = lax.axis_index("dp") * tok_count + jnp.arange(tok_count, dtype=jnp.int32)
    seq_ends = jnp.cumsum(lengths)
    seq_of = jnp.sum((seq_ends[None, :] <= position[:, None]).astype(jnp.int32), axis=1)
    onehot = (seq_of[:, None] == jnp.arange(seq_count, dtype=jnp.int32)[None, :]).astype(
        jnp.float32
    )

    def gram_sum(out_vecs, in_vecs):
        own_rows = lax.dynamic_slice_in_dim(out_vecs, core_index * half_rank, half_rank, 1)
        left = (onehot[:, :, None] * own_rows[:, None, :]).reshape(tok_count, seq_count * half_rank)
        return jnp.dot(left.T, in_vecs, precision=lax.Precision.HIGHEST).reshape(
            seq_count, half_rank, rank_size
        )

    partial_grads = jnp.stack(
        [
            gram_sum(gate_proj, model_proj),
            gram_sum(up_proj, model_proj),
            gram_sum(out_proj, hidden_proj),
        ],
        axis=2,
    )
    partial_grads = partial_grads.reshape(seq_count, half_rank * 3 * rank_size)
    slice_sums = lax.psum_scatter(partial_grads, "dp", scatter_dimension=1, tiled=True)
    slice_grads = slice_sums.astype(jnp.bfloat16)
    scale_rows = 1.0 / jnp.sqrt(lengths.astype(jnp.float32))[:, None]
    query_slice = lax.all_to_all(queries, "dp", split_axis=1, concat_axis=0, tiled=True)
    score_part = contract_rows(slice_grads, query_slice)
    full = lax.psum(score_part, ("dp", "tensor")) * scale_rows
    blocks = full.reshape(seq_count, -1, QBS)
    block_number = blocks.shape[1]
    picker = (cand[:, :, None] == jnp.arange(block_number, dtype=jnp.int32)[None, None, :]).astype(
        jnp.float32
    )
    chosen = jnp.einsum("scb,sbk->sck", picker, blocks, precision=lax.Precision.HIGHEST)
    in_use = jnp.arange(CAND, dtype=jnp.int32)[None, :] < cand_count[:, None]
    return jnp.where(in_use[:, :, None], chosen, jnp.float32(0.0))


def solution(mesh):
    placed = (
        P(("groups", "dp"), "tensor"),
        P(("groups", "dp"), "tensor"),
        P(("groups", "dp"), "tensor"),
        P(("groups", "dp"), "tensor"),
        P(("groups", "dp"), "tensor"),
        P("dp", "tensor"),
        P("dp", "tensor"),
        P("groups"),
        P(("groups", "dp"), "tensor"),
        P("groups", None),
        P("groups"),
    )
    return jax.shard_map(
        local, mesh=mesh, in_specs=placed, out_specs=P("groups", None, None), check_vma=False
    )
```

profile of v0, /device:TPU:0, one launch (start us, length us, event | category | flops | bytes accessed | tf_op | source)
XLA Modules:
  0.0 216.9 jit_solution(13726743882510743481)
XLA Ops:
  6.5 0.0 copy-start
  6.5 0.0 all-gather.2.cloned.1.call-start
  6.5 0.7 all-gather.2.cloned.1.call-update
  7.3 1.8 copy.25
  9.0 7.3 %all-to-all-start = ((bf16[32,8,768]{2,0,1:T(8,128)(2,1)}), bf16[32,8,768]{2,0,1:T(8,128)(2,1)S(1)}, u32[]{:S(2)}, u32[]{:S(2)}) async-start(bf16[32,8,768]{2,0,1:T(8,128)(2,1)} %bitcast.56), calls=%async_computation | async-start | bytes 786432 | tf_op jit(solution)/shard_map/all_to_all | solution.py:87
  16.3 0.0 all-reduce.2.cloned.1.call-start
  16.4 0.8 reduce-window.8
  17.2 0.1 convert_reduce_fusion
  17.3 39.9 %all_gather.6 = bf16[64,4096]{1,0:T(8,128)(2,1)S(1)} all-gather(bf16[8,4096]{1,0:T(8,128)(2,1)} %param.16), channel_id=1, replica_groups=mesh['groups'=2,'dp'=8,'tensor'=2] {'dp'}, dimensions={0}, use_global_device_ids=true | all-gather | bytes 589824 | tf_op jit(solution)/shard_map/all_gather | solution.py:30
  57.2 0.0 copy-done
  57.2 0.4 convolution_dynamic-update-slice_fusion.1
  57.6 8.3 %all-gather.2.cloned.1.call-done = bf16[64,14336]{1,0:T(8,128)(2,1)} async-done(((bf16[8,14336]{1,0:T(8,128)(2,1)}), bf16[64,14336]{1,0:T(8,128)(2,1)}) %all-gather.2.cloned.1.call-update) | async-done | bytes 1835024 | tf_op jit(solution)/shard_map/all_gather | solution.py:31
  65.9 0.0 copy-start.3
  65.9 0.0 copy-start.4
  65.9 0.0 copy-start.5
  65.9 0.0 copy-start.6
  65.9 5.0 %fusion.19 = f32[96,320]{0,1:T(8,128)S(1)} fusion(f32[96,320]{0,1:T(8,128)S(1)} %convolution_dynamic-update-slice_fusion.1, bf16[64,14336]{1,0:T(8,128)(2,1)} %all-gather.2.cloned.1.call-done, bf16[96,14336]{1,0:T(8,128)(2,1)} %param.13, bf16[96,14336]{1,0:T(8,128)(2,1)} %param.12), kind=kOutput, calls=%fused_computation.25 | convolution fusion | flops 187170816 | bytes 7372800 | tf_op jit(solution)/shard_map/dot_general | solution.py:11
  70.9 0.0 copy-done.3
  70.9 0.0 copy-done.4
  71.0 0.5 copy-done.5
  71.5 0.5 copy-done.6
  72.0 2.6 %fusion.16 = f32[96,320]{0,1:T(8,128)S(1)} fusion(f32[96,320]{0,1:T(8,128)S(1)} %fusion.19, bf16[64,14336]{1,0:T(8,128)(2,1)S(1)} %copy-done.6, bf16[96,14336]{1,0:T(8,128)(2,1)S(1)} %copy-done.3, bf16[96,14336]{1,0:T(8,128)(2,1)S(1)} %copy-done.5, bf16[96,14336]{1,0:T(8,128)(2,1)S(1)} %copy-done.4), kind=kOutput, calls=%fused_computation.24 | convolution fusion | flops 194052096 | bytes 10125312 | tf_op jit(solution)/shard_map/dot_general | solution.py:11
  74.6 0.0 copy-start.1
  74.6 0.0 copy-start.8
  74.6 1.8 fusion.22
  76.4 0.0 copy-done.1
  76.4 0.4 convolution_dynamic-update-slice_fusion
  76.8 0.0 copy-start.2
  76.8 0.7 copy-done.2
  77.5 0.0 all-reduce.2.cloned.1.call-update
  77.5 0.0 reduce-scatter.4.cloned.1.call-start
  77.5 0.0 copy-done.8
  77.6 17.7 %all-reduce.2.cloned.1.call-done = f32[96,320]{0,1:T(8,128)} async-done(((f32[96,320]{0,1:T(8,128)}), f32[96,320]{0,1:T(8,128)}) %all-reduce.2.cloned.1.call-update) | async-done | bytes 122896 | tf_op jit(solution)/shard_map/psum | solution.py:50
  95.3 0.8 fusion.44
  96.1 1.0 convolution_bitcast_fusion.1
  97.1 1.0 convolution_bitcast_fusion
  98.0 1.0 convolution_bitcast_fusion.2
  99.0 0.0 copy-start.9
  99.1 0.0 copy-start.7
  99.1 2.3 %copy.21 = f32[4,32,3,64]{0,3,2,1:T(8,128)} copy(f32[4,32,3,64]{3,1,0,2:T(8,128)S(1)} %pad_maximum_fusion) | data formatting | bytes 196608
  101.4 0.0 reduce-scatter.4.cloned.1.call-update
  101.4 0.0 copy-done.9
  101.4 0.1 iota_compare_fusion.3
  101.5 75.5 %reduce-scatter.4.cloned.1.call-done = f32[768,4]{1,0:T(8,128)} async-done(((f32[6144,4]{1,0:T(8,128)}), f32[768,4]{1,0:T(8,128)}) %reduce-scatter.4.cloned.1.call-update) | async-done | bytes 12304
  176.9 1.1 copy.20
  178.1 0.0 all-to-all-done
  178.1 0.2 fusion.45
  178.3 31.1 %psum.15 = f32[4,256]{1,0:T(4,128)S(1)} all-reduce(f32[4,256]{1,0:T(4,128)S(1)} %fusion.45), channel_id=1, replica_groups=mesh['groups'=2,'dp'=8,'tensor'=2] {'dp','tensor'}, use_global_device_ids=true, to_apply=%region_4.5 | all-reduce | flops 1024 | bytes 8192 | tf_op jit(solution)/shard_map/psum | solution.py:89
  209.4 0.1 broadcast_multiply_fusion
  209.5 0.1 reshape.116
  209.6 0.0 copy-done.7
  209.6 0.8 convolution_select_fusion
  (6 shorter events, 0.0 us)
Async XLA Ops:
  6.5 50.7 %copy-start = (bf16[96,4096]{1,0:T(8,128)(2,1)S(1)}, bf16[96,4096]{1,0:T(8,128)(2,1)}, u32[]{:S(2)}) copy-start(bf16[96,4096]{1,0:T(8,128)(2,1)} %param.11) | copy-start | bytes 2359300
  6.5 59.4 %all-gather.2.cloned.1.call-start = ((), (), s32[]{:S(2)}) async-start(), calls=%async_computation.2 | async-start | bytes 2064384 | tf_op jit(solution)/shard_map/all_gather | solution.py:31
  9.0 169.1 %all-to-all-start = ((bf16[32,8,768]{2,0,1:T(8,128)(2,1)}), bf16[32,8,768]{2,0,1:T(8,128)(2,1)S(1)}, u32[]{:S(2)}, u32[]{:S(2)}) async-start(bf16[32,8,768]{2,0,1:T(8,128)(2,1)} %bitcast.56), calls=%async_computation | async-start | bytes 786432 | tf_op jit(solution)/shard_map/all_to_all | solution.py:87
  16.3 79.0 %all-reduce.2.cloned.1.call-start = ((), (), s32[]{:S(2)}) async-start(), calls=%async_computation.3 | async-start | bytes 327680 | tf_op jit(solution)/shard_map/psum | solution.py:50
  65.9 5.0 %copy-start.3 = (bf16[96,14336]{1,0:T(8,128)(2,1)S(1)}, bf16[96,14336]{1,0:T(8,128)(2,1)}, u32[]{:S(2)}) copy-start(bf16[96,14336]{1,0:T(8,128)(2,1)} %param.13) | copy-start | bytes 8257540
  65.9 5.0 %copy-start.4 = (bf16[96,14336]{1,0:T(8,128)(2,1)S(1)}, bf16[96,14336]{1,0:T(8,128)(2,1)}, u32[]{:S(2)}) copy-start(bf16[96,14336]{1,0:T(8,128)(2,1)} %param.12) | copy-start | bytes 8257540
  65.9 5.6 %copy-start.5 = (bf16[96,14336]{1,0:T(8,128)(2,1)S(1)}, bf16[96,14336]{1,0:T(8,128)(2,1)}, u32[]{:S(2)}) copy-start(bf16[96,14336]{1,0:T(8,128)(2,1)} %param.14) | copy-start | bytes 8257540
  65.9 6.1 %copy-start.6 = (bf16[64,14336]{1,0:T(8,128)(2,1)S(1)}, bf16[64,14336]{1,0:T(8,128)(2,1)}, u32[]{:S(2)}) copy-start(bf16[64,14336]{1,0:T(8,128)(2,1)} %all-gather.2.cloned.1.call-done) | copy-start | bytes 5505028
  74.6 1.8 copy-start.1
  74.6 2.9 %copy-start.8 = (s32[4]{0:T(128)S(1)}, s32[4]{0:T(128)}, u32[]{:S(2)}) copy-start(s32[4]{0:T(128)} %param.18) | copy-start | bytes 52
  76.8 0.7 copy-start.2
  77.5 99.5 %reduce-scatter.4.cloned.1.call-start = ((), (), s32[]{:S(2)}) async-start(), calls=%async_computation.4 | async-start | bytes 3538944
  99.0 2.3 %copy-start.9 = (s32[4]{0:T(128)S(1)}, s32[4]{0:T(128)}, u32[]{:S(2)}) copy-start(s32[4]{0:T(128)} %param.21) | copy-start | bytes 52
  99.1 110.5 %copy-start.7 = (s32[4,8]{1,0:T(4,128)S(1)}, s32[4,8]{1,0:T(4,128)}, u32[]{:S(2)}) copy-start(s32[4,8]{1,0:T(4,128)} %param.20) | copy-start | bytes 388
Sparse Core Ops, SparseCore 0:
  9.5 56.3 all-gather.1
  77.6 17.6 all-reduce.1
  101.5 75.3 reduce-scatter.3
where the time goes:
time: 217 us
  waiting for transfers between devices  102 us (47%)
  blocking collectives  71.1 us (33%)
  matrix products  14 us (6%)
  between operations  13.3 us (6%)
  local copies, waits for them, and re-layouts  7.85 us (4%)
  starting transfers between devices  7.36 us (3%)
    unnamed x4, waiting for transfers between devices  76.2 us
    all_gather x1, blocking collectives, local(): lax.all_gather(proj_model, 'dp', axis=0, tiled=True)  39.9 us
    psum x1, blocking collectives, local(): full = lax.psum(score_part, ('dp', 'tensor')) * scale_rows  31.1 us
    psum x1, waiting for transfers between devices, local(): summed = lax.psum(partial_proj, 'tensor')  17.7 us
    dot_general x6, matrix products, contract_rows(): lax.dot_general(left, right, (((1,), (1,)), ((), ())), preferred_element_...  10.3 us
    all_gather x1, waiting for transfers between devices, local(): lax.all_gather(proj_hidden, 'dp', axis=0, tiled=True)  8.3 us
    all_to_all x1, starting transfers between devices, local(): lax.all_to_all(queries, 'dp', split_axis=1, concat_axis=0, tiled=True)  7.28 us
    unnamed x22, local copies, waits for them, and re-layouts  5.18 us
  transfers between devices with their start and end apart: 4, of which 3 were waited for; matrix products, arithmetic and copies ran while one was open for 9% of the time, Pallas kernels for 0%

commit v1 on v0

--- a/solution.py
+++ b/solution.py
@@ -59,7 +59,8 @@
     seq_count = lengths.shape[0]
     tok_count = x_in.shape[0]
     position = lax.axis_index("dp") * tok_count + jnp.arange(tok_count, dtype=jnp.int32)
-    seq_ends = jnp.cumsum(lengths)
+    order = jnp.arange(seq_count, dtype=jnp.int32)
+    seq_ends = jnp.sum(jnp.where(order[None, :] <= order[:, None], lengths[None, :], 0), axis=1)
     seq_of = jnp.sum((seq_ends[None, :] <= position[:, None]).astype(jnp.int32), axis=1)
     onehot = (seq_of[:, None] == jnp.arange(seq_count, dtype=jnp.int32)[None, :]).astype(
         jnp.float32

time: 217 us -> 217 us (level)
  no operation moved by 1% of the time
where the time goes in v1:
time: 217 us
  waiting for transfers between devices  102 us (47%)
  blocking collectives  71.1 us (33%)
  matrix products  14 us (6%)
  between operations  13.3 us (6%)
  local copies, waits for them, and re-layouts  7.85 us (4%)
  starting transfers between devices  7.36 us (3%)
    unnamed x4, waiting for transfers between devices  76.2 us
    all_gather x1, blocking collectives, local(): lax.all_gather(proj_model, 'dp', axis=0, tiled=True)  40 us
    psum x1, blocking collectives, local(): full = lax.psum(score_part, ('dp', 'tensor')) * scale_rows  31.1 us
    psum x1, waiting for transfers between devices, local(): summed = lax.psum(partial_proj, 'tensor')  17.7 us
    dot_general x6, matrix products, contract_rows(): lax.dot_general(left, right, (((1,), (1,)), ((), ())), preferred_element_...  10.3 us
    all_gather x1, waiting for transfers between devices, local(): lax.all_gather(proj_hidden, 'dp', axis=0, tiled=True)  8.3 us
    all_to_all x1, starting transfers between devices, local(): lax.all_to_all(queries, 'dp', split_axis=1, concat_axis=0, tiled=True)  7.28 us
    unnamed x22, local copies, waits for them, and re-layouts  5.18 us
  transfers between devices with their start and end apart: 4, of which 3 were waited for; matrix products, arithmetic and copies ran while one was open for 9% of the time, Pallas kernels for 0%

profile of v1, /device:TPU:0, one launch (start us, length us, event | category | flops | bytes accessed | tf_op | source)
XLA Modules:
  0.0 216.8 jit_solution(6108415900935123091)
XLA Ops:
  6.5 0.0 copy-start
  6.5 0.0 all-gather.2.cloned.1.call-start
  6.5 0.7 all-gather.2.cloned.1.call-update
  7.3 1.8 copy.25
  9.0 7.3 %all-to-all-start = ((bf16[32,8,768]{2,0,1:T(8,128)(2,1)}), bf16[32,8,768]{2,0,1:T(8,128)(2,1)S(1)}, u32[]{:S(2)}, u32[]{:S(2)}) async-start(bf16[32,8,768]{2,0,1:T(8,128)(2,1)} %bitcast.54), calls=%async_computation | async-start | bytes 786432 | tf_op jit(solution)/shard_map/all_to_all | solution.py:88
  16.3 0.0 all-reduce.2.cloned.1.call-start
  16.4 0.8 select_reduce_fusion
  17.1 0.1 convert_reduce_fusion
  17.2 40.0 %all_gather.6 = bf16[64,4096]{1,0:T(8,128)(2,1)S(1)} all-gather(bf16[8,4096]{1,0:T(8,128)(2,1)} %param.16), channel_id=1, replica_groups=mesh['groups'=2,'dp'=8,'tensor'=2] {'dp'}, dimensions={0}, use_global_device_ids=true | all-gather | bytes 589824 | tf_op jit(solution)/shard_map/all_gather | solution.py:30
  57.2 0.0 copy-done
  57.2 0.4 convolution_dynamic-update-slice_fusion.1
  57.6 8.3 %all-gather.2.cloned.1.call-done = bf16[64,14336]{1,0:T(8,128)(2,1)} async-done(((bf16[8,14336]{1,0:T(8,128)(2,1)}), bf16[64,14336]{1,0:T(8,128)(2,1)}) %all-gather.2.cloned.1.call-update) | async-done | bytes 1835024 | tf_op jit(solution)/shard_map/all_gather | solution.py:31
  65.9 0.0 copy-start.3
  65.9 0.0 copy-start.4
  65.9 0.0 copy-start.5
  65.9 0.0 copy-start.6
  65.9 5.0 %fusion.19 = f32[96,320]{0,1:T(8,128)S(1)} fusion(f32[96,320]{0,1:T(8,128)S(1)} %convolution_dynamic-update-slice_fusion.1, bf16[64,14336]{1,0:T(8,128)(2,1)} %all-gather.2.cloned.1.call-done, bf16[96,14336]{1,0:T(8,128)(2,1)} %param.13, bf16[96,14336]{1,0:T(8,128)(2,1)} %param.12), kind=kOutput, calls=%fused_computation.25 | convolution fusion | flops 187170816 | bytes 7372800 | tf_op jit(solution)/shard_map/dot_general | solution.py:11
  70.9 0.0 copy-done.3
  70.9 0.0 copy-done.4
  71.0 0.5 copy-done.5
  71.5 0.5 copy-done.6
  72.0 2.6 %fusion.16 = f32[96,320]{0,1:T(8,128)S(1)} fusion(f32[96,320]{0,1:T(8,128)S(1)} %fusion.19, bf16[64,14336]{1,0:T(8,128)(2,1)S(1)} %copy-done.6, bf16[96,14336]{1,0:T(8,128)(2,1)S(1)} %copy-done.3, bf16[96,14336]{1,0:T(8,128)(2,1)S(1)} %copy-done.5, bf16[96,14336]{1,0:T(8,128)(2,1)S(1)} %copy-done.4), kind=kOutput, calls=%fused_computation.24 | convolution fusion | flops 194052096 | bytes 10125312 | tf_op jit(solution)/shard_map/dot_general | solution.py:11
  74.6 0.0 copy-start.1
  74.6 0.0 copy-start.8
  74.6 1.8 fusion.22
  76.4 0.0 copy-done.1
  76.4 0.4 convolution_dynamic-update-slice_fusion
  76.8 0.0 copy-start.2
  76.8 0.7 copy-done.2
  77.5 0.0 all-reduce.2.cloned.1.call-update
  77.5 0.0 reduce-scatter.4.cloned.1.call-start
  77.5 0.0 copy-done.8
  77.6 17.7 %all-reduce.2.cloned.1.call-done = f32[96,320]{0,1:T(8,128)} async-done(((f32[96,320]{0,1:T(8,128)}), f32[96,320]{0,1:T(8,128)}) %all-reduce.2.cloned.1.call-update) | async-done | bytes 122896 | tf_op jit(solution)/shard_map/psum | solution.py:50
  95.2 0.8 fusion.44
  96.0 1.0 convolution_bitcast_fusion.2
  97.0 1.0 convolution_bitcast_fusion.1
  98.0 1.0 convolution_bitcast_fusion
  99.0 0.0 copy-start.9
  99.0 0.0 copy-start.7
  99.0 2.3 %copy.21 = f32[4,32,3,64]{0,3,2,1:T(8,128)} copy(f32[4,32,3,64]{3,1,0,2:T(8,128)S(1)} %pad_maximum_fusion) | data formatting | bytes 196608
  101.3 0.0 reduce-scatter.4.cloned.1.call-update
  101.3 0.0 copy-done.9
  101.3 0.1 iota_compare_fusion.4
  101.4 75.5 %reduce-scatter.4.cloned.1.call-done = f32[768,4]{1,0:T(8,128)} async-done(((f32[6144,4]{1,0:T(8,128)}), f32[768,4]{1,0:T(8,128)}) %reduce-scatter.4.cloned.1.call-update) | async-done | bytes 12304
  176.8 1.1 copy.20
  178.0 0.0 all-to-all-done
  178.0 0.2 fusion.45
  178.2 31.1 %psum.15 = f32[4,256]{1,0:T(4,128)S(1)} all-reduce(f32[4,256]{1,0:T(4,128)S(1)} %fusion.45), channel_id=1, replica_groups=mesh['groups'=2,'dp'=8,'tensor'=2] {'dp','tensor'}, use_global_device_ids=true, to_apply=%region_4.5 | all-reduce | flops 1024 | bytes 8192 | tf_op jit(solution)/shard_map/psum | solution.py:90
  209.3 0.1 broadcast_multiply_fusion
  209.4 0.1 reshape.92
  209.5 0.0 copy-done.7
  209.5 0.8 convolution_select_fusion
  (6 shorter events, 0.0 us)
Async XLA Ops:
  6.5 50.7 %copy-start = (bf16[96,4096]{1,0:T(8,128)(2,1)S(1)}, bf16[96,4096]{1,0:T(8,128)(2,1)}, u32[]{:S(2)}) copy-start(bf16[96,4096]{1,0:T(8,128)(2,1)} %param.11) | copy-start | bytes 2359300
  6.5 59.4 %all-gather.2.cloned.1.call-start = ((), (), s32[]{:S(2)}) async-start(), calls=%async_computation.2 | async-start | bytes 2064384 | tf_op jit(solution)/shard_map/all_gather | solution.py:31
  9.0 169.0 %all-to-all-start = ((bf16[32,8,768]{2,0,1:T(8,128)(2,1)}), bf16[32,8,768]{2,0,1:T(8,128)(2,1)S(1)}, u32[]{:S(2)}, u32[]{:S(2)}) async-start(bf16[32,8,768]{2,0,1:T(8,128)(2,1)} %bitcast.54), calls=%async_computation | async-start | bytes 786432 | tf_op jit(solution)/shard_map/all_to_all | solution.py:88
  16.3 78.9 %all-reduce.2.cloned.1.call-start = ((), (), s32[]{:S(2)}) async-start(), calls=%async_computation.3 | async-start | bytes 327680 | tf_op jit(solution)/shard_map/psum | solution.py:50
  65.9 5.0 %copy-start.3 = (bf16[96,14336]{1,0:T(8,128)(2,1)S(1)}, bf16[96,14336]{1,0:T(8,128)(2,1)}, u32[]{:S(2)}) copy-start(bf16[96,14336]{1,0:T(8,128)(2,1)} %param.13) | copy-start | bytes 8257540
  65.9 5.0 %copy-start.4 = (bf16[96,14336]{1,0:T(8,128)(2,1)S(1)}, bf16[96,14336]{1,0:T(8,128)(2,1)}, u32[]{:S(2)}) copy-start(bf16[96,14336]{1,0:T(8,128)(2,1)} %param.12) | copy-start | bytes 8257540
  65.9 5.6 %copy-start.5 = (bf16[96,14336]{1,0:T(8,128)(2,1)S(1)}, bf16[96,14336]{1,0:T(8,128)(2,1)}, u32[]{:S(2)}) copy-start(bf16[96,14336]{1,0:T(8,128)(2,1)} %param.14) | copy-start | bytes 8257540
  65.9 6.1 %copy-start.6 = (bf16[64,14336]{1,0:T(8,128)(2,1)S(1)}, bf16[64,14336]{1,0:T(8,128)(2,1)}, u32[]{:S(2)}) copy-start(bf16[64,14336]{1,0:T(8,128)(2,1)} %all-gather.2.cloned.1.call-done) | copy-start | bytes 5505028
  74.6 1.8 copy-start.1
  74.6 2.9 %copy-start.8 = (s32[4]{0:T(128)S(1)}, s32[4]{0:T(128)}, u32[]{:S(2)}) copy-start(s32[4]{0:T(128)} %param.18) | copy-start | bytes 52
  76.8 0.7 copy-start.2
  77.5 99.4 %reduce-scatter.4.cloned.1.call-start = ((), (), s32[]{:S(2)}) async-start(), calls=%async_computation.4 | async-start | bytes 3538944
  99.0 2.3 %copy-start.9 = (s32[4]{0:T(128)S(1)}, s32[4]{0:T(128)}, u32[]{:S(2)}) copy-start(s32[4]{0:T(128)} %param.21) | copy-start | bytes 52
  99.0 110.5 %copy-start.7 = (s32[4,8]{1,0:T(4,128)S(1)}, s32[4,8]{1,0:T(4,128)}, u32[]{:S(2)}) copy-start(s32[4,8]{1,0:T(4,128)} %param.20) | copy-start | bytes 388
Sparse Core Ops, SparseCore 0:
  9.5 56.3 all-gather.1
  77.6 17.5 all-reduce.1
  101.4 75.3 reduce-scatter.3

commit v2 on v0

v2 whole, which is shorter than its diff:
```python
import functools
import jax
import jax.numpy as jnp
from jax import lax
from jax.experimental import pallas as pl
from jax.experimental.pallas import tpu as pltpu
from jax.sharding import PartitionSpec as P

MESH = pl.DeviceIdType.MESH
F32 = jnp.float32
BF16 = jnp.bfloat16
LANES = 128
FOLDED = 16
CHUNKS = 3
SHARE = 0.36


def iota(shape, dim):
    return lax.broadcasted_iota(jnp.int32, shape, dim)


def dot_nt(left, right):
    return lax.dot_general(left, right, (((1,), (1,)), ((), ())), preferred_element_type=F32)


def dot_nn(left, right):
    return lax.dot_general(left, right, (((1,), (0,)), ((), ())), preferred_element_type=F32)


def halves(value):
    high = value.astype(BF16)
    return high, (value - high.astype(F32)).astype(BF16)


def kernel(
    dims,
    len_ref, cand_ref, count_ref,
    x_hbm, gate_hbm, up_hbm, grad_hbm, out_hbm, pm_hbm, ph_hbm, q_hbm,
    o_ref,
    gate, up, grad, act, xo, pm, ph, q, qr, w, acc_h, acc_m,
    proj, proj_other, parts, parts_in, sg, flat, finals,
    sem_in, sem_small, s_right, s_left, s_y, s_x, r_zy, r_x,
    s_pair, r_pair, s_rs, r_rs, s_ag, r_ag, s_fin, r_fin,
):
    groups, dp, tp, rows, seqs, cands = dims
    toks, ffl = gate.shape
    ml = pm.shape[1]
    fold = FOLDED // rows
    rank = rows * dp
    mfold, hfold = ml // fold, ffl // fold
    width = mfold + hfold
    chunk = width // CHUNKS
    blocks = chunk // LANES
    part = LANES * max(1, round(blocks * SHARE))
    zs = dp // 2
    half = rank // tp
    il = half // dp
    n_in = sem_in.shape[1]
    in_cols = ffl // n_in

    g = lax.axis_index("groups")
    me = lax.axis_index("dp")
    core = lax.axis_index("tensor")
    z, y = me // 2, lax.rem(me, 2)
    xx = lax.rem(g, 2)
    other_g = g + 1 - 2 * xx
    other_core = lax.rem(core + 1, tp)

    small = [
        pltpu.make_async_copy(pm_hbm, pm, sem_small.at[0]),
        pltpu.make_async_copy(ph_hbm, ph, sem_small.at[1]),
        pltpu.make_async_copy(x_hbm, xo.at[pl.ds(0, toks)], sem_small.at[2]),
        pltpu.make_async_copy(out_hbm, xo.at[pl.ds(toks, toks)], sem_small.at[3]),
        pltpu.make_async_copy(q_hbm, q, sem_small.at[4]),
    ]
    small[0].start()
    small[1].start()

    barrier = pltpu.get_barrier_semaphore()
    for step in range(1, dp * tp):
        flat_id = lax.rem(me * tp + core + step, dp * tp)
        pl.semaphore_signal(
            barrier, inc=1, device_id={"dp": flat_id // tp, "tensor": lax.rem(flat_id, tp)}, device_id_type=MESH
        )
    pl.semaphore_signal(barrier, inc=1, device_id={"groups": other_g}, device_id_type=MESH)

    def big(n, which):
        src, dst = ((gate_hbm, gate), (up_hbm, up), (grad_hbm, grad))[which]
        cols = pl.ds(n * in_cols, in_cols)
        return pltpu.make_async_copy(src.at[:, cols], dst.at[:, cols], sem_in.at[which, n])

    for n in range(n_in):
        for which in range(3):
            big(n, which).start()
    for c in small[2:]:
        c.start()

    small[0].wait()
    small[1].wait()
    mine = w.at[me]
    for src, cols, base in ((pm, mfold, 0), (ph, hfold, mfold)):
        mine[:, base : base + cols] = jnp.concatenate(
            [src[:, f * cols : (f + 1) * cols].astype(F32) for f in range(fold)], axis=0
        ).astype(BF16)
    pl.semaphore_wait(barrier, dp * tp)

    zy_cols = [pl.ds(pl.multiple_of(c * chunk + xx * part, LANES), chunk - part) for c in range(CHUNKS)]
    x_cols = [pl.ds(pl.multiple_of(c * chunk + xx * (chunk - part), LANES), part) for c in range(CHUNKS)]
    x_in_cols = [pl.ds(pl.multiple_of(c * chunk + (1 - xx) * (chunk - part), LANES), part) for c in range(CHUNKS)]

    def zy_copy(c, slot, send_sem, target):
        ref = w.at[slot, :, zy_cols[c]]
        return pltpu.make_async_remote_copy(ref, ref, send_sem, r_zy.at[c, slot], device_id=target, device_id_type=MESH)

    def x_copy(c, slot, send_sem, cols):
        ref = w.at[slot, :, cols[c]]
        return pltpu.make_async_remote_copy(
            ref, ref, send_sem, r_x.at[c, slot], device_id={"groups": other_g}, device_id_type=MESH
        )

    def slot_of(pos, col):
        return jnp.clip(pos, 0, zs - 1) * 2 + col

    def right_send(c, k):
        return zy_copy(c, slot_of(z - k, y), s_right.at[c, k], {"dp": me + 2})

    def left_send(c, k):
        return zy_copy(c, slot_of(z + k, y), s_left.at[c, k], {"dp": me - 2})

    def y_send(c, k, way):
        return zy_copy(c, slot_of(z + way * k, y), s_y.at[c, zs + way * k], {"dp": z * 2 + 1 - y})

    def x_send(c, k, way, col):
        return x_copy(c, slot_of(z + way * k, jnp.where(col == 0, y, 1 - y)), s_x.at[c, col, zs + way * k], x_cols)

    def own_step(c):
        @pl.when(z + 1 < zs)
        def _():
            right_send(c, 0).start()

        @pl.when(z >= 1)
        def _():
            left_send(c, 0).start()

        y_send(c, 0, 1).start()

    def z_step(c, k):
        @pl.when(z - k >= 0)
        def _():
            right_send(c, k).wait_recv()

            @pl.when(z + 1 < zs)
            def _():
                right_send(c, k).start()

            y_send(c, k, -1).start()
            x_send(c, k, -1, 0).start()

        @pl.when(z + k < zs)
        def _():
            left_send(c, k).wait_recv()

            @pl.when(z >= 1)
            def _():
                left_send(c, k).start()

            y_send(c, k, 1).start()
            x_send(c, k, 1, 0).start()

    def y_step(c, k):
        for way in (-1, 1) if k else (1,):

            @pl.when((z + way * k >= 0) & (z + way * k < zs))
            def _():
                slot = slot_of(z + way * k, 1 - y)
                zy_copy(c, slot, s_y.at[c, zs], {"dp": me}).wait_recv()
                x_send(c, k, way, 1).start()

    def x_wait(c):
        for step in range(1, dp):
            x_copy(c, lax.rem(me + step, dp), s_x.at[c, 0, zs], x_in_cols).wait_recv()

    for c in range(CHUNKS):
        own_step(c)

    step_cols = 4 * LANES
    while in_cols % step_cols:
        step_cols //= 2
    acts = ffl // step_cols

    def activate(base):
        for r in range(0, toks, FOLDED):
            at = (pl.ds(r, FOLDED), pl.ds(base, step_cols))
            gv, uv, dv = gate[at].astype(F32), up[at].astype(F32), grad[at].astype(F32)
            sig = 0.5 * jnp.tanh(0.5 * gv) + 0.5
            silu = gv * sig
            act[pl.ds(r, FOLDED), pl.ds(base, step_cols)] = (silu * uv).astype(BF16)
            act[pl.ds(toks + r, FOLDED), pl.ds(base, step_cols)] = (
                dv * uv * (sig * (1.0 + gv * (1.0 - sig)))
            ).astype(BF16)
            act[pl.ds(2 * toks + r, FOLDED), pl.ds(base, step_cols)] = (dv * silu).astype(BF16)

    def activate_input(n):
        for which in range(3):
            big(n, which).wait()

        @pl.loop(0, in_cols // step_cols)
        def _(i):
            activate(pl.multiple_of(n * in_cols + i * step_cols, LANES))

    def spread_queries():
        small[4].wait()
        qs = q.shape[0]
        wide = q.shape[1] // half
        for i in range(half):
            qr[i * qs : (i + 1) * qs, :] = q[:, i * wide : (i + 1) * wide]

    events = []
    for k in range(zs):
        if k:
            events += [functools.partial(z_step, c, k) for c in range(CHUNKS)]
            events += [functools.partial(y_step, c, k - 1) for c in range(CHUNKS)]
    last = [functools.partial(y_step, c, zs - 1) for c in range(CHUNKS)]

    work = [functools.partial(activate_input, n) for n in range(n_in)] + [spread_queries]
    done = 0
    for n, job in enumerate(work):
        job()
        upto = (n + 1) * len(events) // len(work)
        for e in events[done:upto]:
            e()
        done = upto

    acc_h[...] = jnp.zeros_like(acc_h)
    acc_m[...] = jnp.zeros_like(acc_m)
    lanes_w = dp * FOLDED
    small[2].wait()
    small[3].wait()

    def multiply(acc, src, total, lo, hi, base):
        if hi <= lo:
            return
        kc = 4 * LANES
        while (hi - lo) % kc:
            kc //= 2

        @pl.loop(0, (hi - lo) // kc)
        def _(i):
            at = lo + i * kc
            wv = w[:, :, pl.ds(pl.multiple_of(base + at, LANES), kc)].reshape(lanes_w, kc)
            for f in range(fold):
                sv = src[:, pl.ds(pl.multiple_of(f * total + at, LANES), kc)]
                acc[f] += dot_nt(sv, wv)

    def multiply_chunk(c):
        x_wait(c)
        lo, hi = c * chunk, (c + 1) * chunk
        multiply(acc_m, xo, mfold, lo, min(hi, mfold), 0)
        multiply(acc_h, act, hfold, max(lo - mfold, 0), hi - mfold, mfold)

    last[0]()
    for c in range(CHUNKS):
        if c + 1 < CHUNKS:
            last[c + 1]()
        multiply_chunk(c)

    lane, col = iota((lanes_w, rank), 0), iota((lanes_w, rank), 1)
    for acc, base in ((acc_h, 0), (acc_m, 3 * toks)):
        total = None
        for f in range(fold):
            local = lax.rem(lane, FOLDED) - f * rows
            pick = ((lane // FOLDED) * rows + local == col) & (local >= 0) & (local < rows)
            pick = pick.astype(F32).astype(BF16)
            high, low = halves(acc[f])
            term = dot_nn(high, pick) + dot_nn(low, pick)
            total = term if total is None else total + term
        proj[pl.ds(base, acc.shape[1]), :] = total
    pair = pltpu.make_async_remote_copy(
        proj, proj_other, s_pair, r_pair, device_id={"tensor": other_core}, device_id_type=MESH
    )
    pair.start()

    n_rows = seqs * half
    slice_rows = seqs * il
    rr = iota((n_rows, toks), 0)
    seq_of_row = lax.rem(rr, slice_rows) // il
    position = me * toks + iota((n_rows, toks), 1)
    start = jnp.int32(0)
    inside = jnp.zeros((n_rows, toks), jnp.bool_)
    for s in range(seqs):
        stop = start + len_ref[s]
        inside = inside | ((seq_of_row == s) & (position >= start) & (position < stop))
        start = stop
    r2, c2 = iota((n_rows, rank), 0), iota((n_rows, rank), 1)
    chosen_rank = core * half + (r2 // slice_rows) * il + lax.rem(r2, il)
    pick_left = (c2 == chosen_rank).astype(F32).astype(BF16)
    pair.wait()

    def vectors(m):
        at = pl.ds(m * toks, toks)
        return proj[at, :] + proj_other[at, :]

    hidden_v, gate_v, up_v, model_v, out_v = [vectors(m) for m in range(5)]
    for m, (a, b) in enumerate(((gate_v, model_v), (up_v, model_v), (out_v, hidden_v))):
        high, low = halves(a)
        left = jnp.where(inside, dot_nt(pick_left, high) + dot_nt(pick_left, low), 0.0)
        lh, ll = halves(left)
        bh, bl = halves(b)
        gram = dot_nn(lh, bh) + (dot_nn(lh, bl) + dot_nn(ll, bh))
        for d in range(dp):
            parts[d, :, m * rank : (m + 1) * rank] = gram[d * slice_rows : (d + 1) * slice_rows]

    def rs(step):
        to = lax.rem(me + step, dp)
        return pltpu.make_async_remote_copy(
            parts.at[to], parts_in.at[step], s_rs.at[step], r_rs.at[step], device_id={"dp": to}, device_id_type=MESH
        )

    def ag(step):
        return pltpu.make_async_remote_copy(
            sg.at[0], sg.at[step], s_ag.at[step], r_ag.at[step],
            device_id={"dp": lax.rem(me + step, dp)}, device_id_type=MESH,
        )

    for step in range(1, dp):
        rs(step).start()
    total = parts[me]
    for step in range(1, dp):
        rs(step).wait_recv()
        total = total + parts_in[step]
    sg[0] = total.astype(BF16).astype(F32)
    for step in range(1, dp):
        ag(step).start()
    flat[0:slice_rows, :] = sg[0]
    for step in range(1, dp):
        ag(step).wait_recv()
        flat[step * slice_rows : (step + 1) * slice_rows, :] = sg[step]

    qs = q.shape[0]
    big_scores = dot_nt(flat[...].astype(BF16), qr[...])
    br, bc = iota(big_scores.shape, 0), iota(big_scores.shape, 1)
    from_dev = lax.rem(me + dp - br // slice_rows, dp)
    same = (from_dev * il + lax.rem(br, il)) == bc // qs
    high, low = halves(jnp.where(same, big_scores, 0.0))
    sr, sc = iota((8, n_rows), 0), iota((8, n_rows), 1)
    sum_rows = (lax.rem(sc, slice_rows) // il == sr).astype(F32).astype(BF16)
    by_seq = dot_nn(sum_rows, high) + dot_nn(sum_rows, low)
    fr, fc = iota((half * qs, LANES), 0), iota((half * qs, LANES), 1)
    fold_q = (lax.rem(fr, qs) == fc).astype(F32).astype(BF16)
    high, low = halves(by_seq)
    finals[me * tp + core] = dot_nn(high, fold_q) + dot_nn(low, fold_q)

    def fin(step):
        mine = me * tp + core
        to = lax.rem(mine + step, dp * tp)
        return pltpu.make_async_remote_copy(
            finals.at[mine], finals.at[mine], s_fin.at[step], r_fin.at[step],
            device_id={"dp": to // tp, "tensor": lax.rem(to, tp)}, device_id_type=MESH,
        )

    for step in range(1, dp * tp):
        fin(step).start()

    row = iota((8, LANES), 0)
    lens = jnp.ones((8, LANES), F32)
    for s in range(seqs):
        lens = jnp.where(row == s, len_ref[s].astype(F32), lens)
    scale = 1.0 / jnp.sqrt(lens)
    wanted = []
    for c in range(cands):
        v = jnp.full((8, LANES), -1, jnp.int32)
        for s in range(seqs):
            v = jnp.where(row == s, jnp.where(c < count_ref[s], cand_ref[s, c], -1), v)
        wanted.append(v)
    for step in range(1, dp * tp):
        fin(step).wait_recv()
    found = [jnp.zeros((8, LANES), F32) for _ in range(cands)]
    for b in range(dp):
        block = finals[b * tp]
        for t in range(1, tp):
            block = block + finals[b * tp + t]
        block = block * scale
        for c in range(cands):
            found[c] = jnp.where(wanted[c] == b, block, found[c])
    for c in range(cands):
        o_ref[:, c, :] = found[c][:seqs, :qs]

    for step in range(1, dp * tp):
        fin(step).wait_send()
    for step in range(1, dp):
        rs(step).wait_send()
        ag(step).wait_send()
    for c in range(CHUNKS):
        for k in range(zs):

            @pl.when((z - k >= 0) & (z + 1 < zs))
            def _():
                right_send(c, k).wait_send()

            @pl.when((z + k < zs) & (z >= 1))
            def _():
                left_send(c, k).wait_send()

            for way in (-1, 1) if k else (1,):

                @pl.when((z + way * k >= 0) & (z + way * k < zs))
                def _():
                    y_send(c, k, way).wait_send()
                    x_send(c, k, way, 1).wait_send()
                    if k:
                        x_send(c, k, way, 0).wait_send()


def local(groups, dp, tp, x_in, gate_pre, up_pre, grad_hidden, grad_out, proj_model, proj_hidden, lengths, queries, cand, cand_count):
    toks, ffl = gate_pre.shape
    rows, ml = proj_model.shape
    seqs, cands = cand.shape
    qs, feats = queries.shape
    rank = rows * dp
    half = rank // tp
    fold = FOLDED // rows
    width = (ml + ffl) // fold
    zs = dp // 2
    slice_rows = seqs * (half // dp)
    n_in = 7
    dma = pltpu.SemaphoreType.DMA
    any_spec = pl.BlockSpec(memory_space=pl.ANY)
    smem = pl.BlockSpec(memory_space=pltpu.SMEM)
    return pl.pallas_call(
        functools.partial(kernel, (groups, dp, tp, rows, seqs, cands)),
        out_shape=jax.ShapeDtypeStruct((seqs, cands, qs), F32),
        in_specs=[smem] * 3 + [any_spec] * 8,
        out_specs=pl.BlockSpec(memory_space=pltpu.VMEM),
        scratch_shapes=[
            pltpu.VMEM((toks, ffl), BF16),
            pltpu.VMEM((toks, ffl), BF16),
            pltpu.VMEM((toks, ffl), BF16),
            pltpu.VMEM((3 * toks, ffl), BF16),
            pltpu.VMEM((2 * toks, ml), BF16),
            pltpu.VMEM((rows, ml), BF16),
            pltpu.VMEM((rows, ffl), BF16),
            pltpu.VMEM((qs, feats), BF16),
            pltpu.VMEM((half * qs, feats // half), BF16),
            pltpu.VMEM((dp, FOLDED, width), BF16),
            pltpu.VMEM((fold, 3 * toks, dp * FOLDED), F32),
            pltpu.VMEM((fold, 2 * toks, dp * FOLDED), F32),
            pltpu.VMEM((5 * toks, rank), F32),
            pltpu.VMEM((5 * toks, rank), F32),
            pltpu.VMEM((dp, slice_rows, 3 * rank), F32),
            pltpu.VMEM((dp, slice_rows, 3 * rank), F32),
            pltpu.VMEM((dp, slice_rows, 3 * rank), F32),
            pltpu.VMEM((seqs * half, 3 * rank), F32),
            pltpu.VMEM((dp * tp, 8, LANES), F32),
            dma((3, n_in)),
            dma((5,)),
            dma((CHUNKS, zs)),
            dma((CHUNKS, zs)),
            dma((CHUNKS, 2 * zs)),
            dma((CHUNKS, 2, 2 * zs)),
            dma((CHUNKS, dp)),
            dma((CHUNKS, dp)),
            dma,
            dma,
            dma((dp,)),
            dma((dp,)),
            dma((dp,)),
            dma((dp,)),
            dma((dp * tp,)),
            dma((dp * tp,)),
        ],
        compiler_params=pltpu.CompilerParams(
            collective_id=0, has_side_effects=True, vmem_limit_bytes=56 * 1024 * 1024
        ),
    )(lengths, cand, cand_count, x_in, gate_pre, up_pre, grad_hidden, grad_out, proj_model, proj_hidden, queries)


def solution(mesh):
    placed = (
        P(("groups", "dp"), "tensor"),
        P(("groups", "dp"), "tensor"),
        P(("groups", "dp"), "tensor"),
        P(("groups", "dp"), "tensor"),
        P(("groups", "dp"), "tensor"),
        P("dp", "tensor"),
        P("dp", "tensor"),
        P("groups"),
        P(("groups", "dp"), "tensor"),
        P("groups", None),
        P("groups"),
    )
    sizes = mesh.shape
    return jax.shard_map(
        functools.partial(local, sizes["groups"], sizes["dp"], sizes["tensor"]),
        mesh=mesh, in_specs=placed, out_specs=P("groups", None, None), check_vma=False,
    )
```

time: 217 us -> 54.8 us (0.25)
  waiting for transfers between devices: 102 us -> 0 us
  blocking collectives: 71.1 us -> 0 us
  Pallas kernels: 0 us -> 53.2 us
  matrix products: 14 us -> 0 us
  between operations: 13.3 us -> 0.01 us
  starting transfers between devices: 7.36 us -> 0 us
  local copies, waits for them, and re-layouts: 7.85 us -> 1.32 us
    unnamed x4 -> x0, waiting for transfers between devices: 76.2 us -> none
    pallas_call x0 -> x1, Pallas kernels: none -> 53.2 us  [local(): pl.pallas_call(functools.partial(kernel, (groups, dp, tp, rows, seqs, can...]
    all_gather x1 -> x0, blocking collectives: 39.9 us -> none  [local(): lax.all_gather(proj_model, 'dp', axis=0, tiled=True)]
    psum x1 -> x0, blocking collectives: 31.1 us -> none  [local(): full = lax.psum(score_part, ('dp', 'tensor')) * scale_rows]
    psum x1 -> x0, waiting for transfers between devices: 17.7 us -> none  [local(): summed = lax.psum(partial_proj, 'tensor')]
    dot_general x10 -> x0, matrix products: 14 us -> none  [the longest x6 10.3 us: contract_rows(): lax.dot_general(left, right, (((1,), (1,)), ((), ())), preferred_element_...]
    all_gather x1 -> x0, waiting for transfers between devices: 8.3 us -> none  [local(): lax.all_gather(proj_hidden, 'dp', axis=0, tiled=True)]
    all_to_all x1 -> x0, starting transfers between devices: 7.28 us -> none  [local(): lax.all_to_all(queries, 'dp', split_axis=1, concat_axis=0, tiled=True)]
  transfers between devices with their start and end apart: 4 -> 0, of which waited for: 3 -> 0; matrix products, arithmetic and copies ran while one was open for 9% -> 0% of each run, Pallas kernels for 0% -> 0%
where the time goes in v2:
time: 54.8 us; the launch traced here: 54.5 us
  Pallas kernels  53.2 us (97%)
  local copies, waits for them, and re-layouts  1.32 us (2%)
    pallas_call x1, Pallas kernels, local(): pl.pallas_call(functools.partial(kernel, (groups, dp, tp, rows, seqs, can...  53.2 us
    unnamed x1, local copies, waits for them, and re-layouts  1.32 us

profile of v2, /device:TPU:0, one launch (start us, length us, event | category | flops | bytes accessed | tf_op | source)
XLA Modules:
  0.0 54.5 jit_solution(18275824254877792893)
XLA Ops:
  0.0 53.2 %shard_map.109 = f32[4,8,32]{2,1,0:T(8,128)} custom-call(s32[4]{0:T(128)} %len_ref.1, s32[4,8]{1,0:T(4,128)} %cand_ref.1, s32[4]{0:T(128)} %count_ref.1, bf16[96,4096]{1,0:T(8,128)(2,1)} %x_hbm.1, bf16[96,14336]{1,0:T(8,128)(2,1)} %gate_hbm.1, bf16[96,14336]{1,0:T(8,128)(2,1)} %up_hbm.1, bf16[96,14336]{1,0:T(8,128)(2,1)} %grad_hbm.1, ...), custom_call_target="tpu_custom_call" | custom-call | tf_op jit(solution)/shard_map/pallas_call | solution.py:429
  53.2 1.3 %copy.13 = f32[4,8,32]{2,1,0:T(8,128)} copy(f32[4,8,32]{2,1,0:T(8,128)} %shard_map.109) | data formatting | bytes 8192

commit v3 on v2

--- a/solution.py
+++ b/solution.py
@@ -11,8 +11,8 @@
 BF16 = jnp.bfloat16
 LANES = 128
 FOLDED = 16
-CHUNKS = 3
-SHARE = 0.36
+CHUNKS = 2
+SHARE = 0.3
 
 
 def iota(shape, dim):
@@ -38,7 +38,7 @@
     x_hbm, gate_hbm, up_hbm, grad_hbm, out_hbm, pm_hbm, ph_hbm, q_hbm,
     o_ref,
     gate, up, grad, act, xo, pm, ph, q, qr, w, acc_h, acc_m,
-    proj, proj_other, parts, parts_in, sg, flat, finals,
+    proj, proj_other, parts, parts_in, sg, flat, halved, finals,
     sem_in, sem_small, s_right, s_left, s_y, s_x, r_zy, r_x,
     s_pair, r_pair, s_rs, r_rs, s_ag, r_ag, s_fin, r_fin,
 ):
@@ -77,12 +77,16 @@
     small[1].start()
 
     barrier = pltpu.get_barrier_semaphore()
-    for step in range(1, dp * tp):
-        flat_id = lax.rem(me * tp + core + step, dp * tp)
-        pl.semaphore_signal(
-            barrier, inc=1, device_id={"dp": flat_id // tp, "tensor": lax.rem(flat_id, tp)}, device_id_type=MESH
-        )
-    pl.semaphore_signal(barrier, inc=1, device_id={"groups": other_g}, device_id_type=MESH)
+    for target in ({"dp": z * 2 + 1 - y}, {"groups": other_g}, {"tensor": other_core}):
+        pl.semaphore_signal(barrier, inc=1, device_id=target, device_id_type=MESH)
+
+    @pl.when(z + 1 < zs)
+    def _():
+        pl.semaphore_signal(barrier, inc=1, device_id={"dp": me + 2}, device_id_type=MESH)
+
+    @pl.when(z >= 1)
+    def _():
+        pl.semaphore_signal(barrier, inc=1, device_id={"dp": me - 2}, device_id_type=MESH)
 
     def big(n, which):
         src, dst = ((gate_hbm, gate), (up_hbm, up), (grad_hbm, grad))[which]
@@ -102,7 +106,7 @@
         mine[:, base : base + cols] = jnp.concatenate(
             [src[:, f * cols : (f + 1) * cols].astype(F32) for f in range(fold)], axis=0
         ).astype(BF16)
-    pl.semaphore_wait(barrier, dp * tp)
+    pl.semaphore_wait(barrier, 3 + (z + 1 < zs).astype(jnp.int32) + (z >= 1).astype(jnp.int32))
 
     zy_cols = [pl.ds(pl.multiple_of(c * chunk + xx * part, LANES), chunk - part) for c in range(CHUNKS)]
     x_cols = [pl.ds(pl.multiple_of(c * chunk + xx * (chunk - part), LANES), part) for c in range(CHUNKS)]
@@ -240,9 +244,8 @@
     def multiply(acc, src, total, lo, hi, base):
         if hi <= lo:
             return
-        kc = 4 * LANES
-        while (hi - lo) % kc:
-            kc //= 2
+        units = (hi - lo) // LANES
+        kc = LANES * max(n for n in range(1, 13) if units % n == 0)
 
         @pl.loop(0, (hi - lo) // kc)
         def _(i):
@@ -276,7 +279,7 @@
             total = term if total is None else total + term
         proj[pl.ds(base, acc.shape[1]), :] = total
     pair = pltpu.make_async_remote_copy(
-        proj, proj_other, s_pair, r_pair, device_id={"tensor": other_core}, device_id_type=MESH
+        proj, proj_other, s_pair.at[0], r_pair.at[0], device_id={"tensor": other_core}, device_id_type=MESH
     )
     pair.start()
 
@@ -308,7 +311,7 @@
         bh, bl = halves(b)
         gram = dot_nn(lh, bh) + (dot_nn(lh, bl) + dot_nn(ll, bh))
         for d in range(dp):
-            parts[d, :, m * rank : (m + 1) * rank] = gram[d * slice_rows : (d + 1) * slice_rows]
+            parts[d, :, m * rank : (m + 1) * rank] = gram[d * slice_rows : (d + 1) * slice_rows].astype(BF16)
 
     def rs(step):
         to = lax.rem(me + step, dp)
@@ -324,11 +327,11 @@
 
     for step in range(1, dp):
         rs(step).start()
-    total = parts[me]
+    total = parts[me].astype(F32)
     for step in range(1, dp):
         rs(step).wait_recv()
-        total = total + parts_in[step]
-    sg[0] = total.astype(BF16).astype(F32)
+        total = total + parts_in[step].astype(F32)
+    sg[0] = total.astype(BF16)
     for step in range(1, dp):
         ag(step).start()
     flat[0:slice_rows, :] = sg[0]
@@ -337,7 +340,7 @@
         flat[step * slice_rows : (step + 1) * slice_rows, :] = sg[step]
 
     qs = q.shape[0]
-    big_scores = dot_nt(flat[...].astype(BF16), qr[...])
+    big_scores = dot_nt(flat[...], qr[...])
     br, bc = iota(big_scores.shape, 0), iota(big_scores.shape, 1)
     from_dev = lax.rem(me + dp - br // slice_rows, dp)
     same = (from_dev * il + lax.rem(br, il)) == bc // qs
@@ -348,18 +351,17 @@
     fr, fc = iota((half * qs, LANES), 0), iota((half * qs, LANES), 1)
     fold_q = (lax.rem(fr, qs) == fc).astype(F32).astype(BF16)
     high, low = halves(by_seq)
-    finals[me * tp + core] = dot_nn(high, fold_q) + dot_nn(low, fold_q)
+    halved[0] = dot_nn(high, fold_q) + dot_nn(low, fold_q)
+    score_pair = pltpu.make_async_remote_copy(
+        halved.at[0], halved.at[1], s_pair.at[1], r_pair.at[1], device_id={"tensor": other_core}, device_id_type=MESH
+    )
+    score_pair.start()
 
     def fin(step):
-        mine = me * tp + core
-        to = lax.rem(mine + step, dp * tp)
         return pltpu.make_async_remote_copy(
-            finals.at[mine], finals.at[mine], s_fin.at[step], r_fin.at[step],
-            device_id={"dp": to // tp, "tensor": lax.rem(to, tp)}, device_id_type=MESH,
+            finals.at[0], finals.at[step], s_fin.at[step], r_fin.at[step],
+            device_id={"dp": lax.rem(me + step, dp)}, device_id_type=MESH,
         )
-
-    for step in range(1, dp * tp):
-        fin(step).start()
 
     row = iota((8, LANES), 0)
     lens = jnp.ones((8, LANES), F32)
@@ -372,22 +374,23 @@
         for s in range(seqs):
             v = jnp.where(row == s, jnp.where(c < count_ref[s], cand_ref[s, c], -1), v)
         wanted.append(v)
-    for step in range(1, dp * tp):
-        fin(step).wait_recv()
     found = [jnp.zeros((8, LANES), F32) for _ in range(cands)]
-    for b in range(dp):
-        block = finals[b * tp]
-        for t in range(1, tp):
-            block = block + finals[b * tp + t]
-        block = block * scale
+    score_pair.wait()
+    finals[0] = (halved[0] + halved[1]) * scale
+    for step in range(1, dp):
+        fin(step).start()
+    for step in range(dp):
+        if step:
+            fin(step).wait_recv()
+        block = finals[step]
+        b = lax.rem(me + dp - step, dp)
         for c in range(cands):
             found[c] = jnp.where(wanted[c] == b, block, found[c])
     for c in range(cands):
         o_ref[:, c, :] = found[c][:seqs, :qs]
 
-    for step in range(1, dp * tp):
+    for step in range(1, dp):
         fin(step).wait_send()
-    for step in range(1, dp):
         rs(step).wait_send()
         ag(step).wait_send()
     for c in range(CHUNKS):
@@ -446,11 +449,12 @@
             pltpu.VMEM((fold, 2 * toks, dp * FOLDED), F32),
             pltpu.VMEM((5 * toks, rank), F32),
             pltpu.VMEM((5 * toks, rank), F32),
-            pltpu.VMEM((dp, slice_rows, 3 * rank), F32),
-            pltpu.VMEM((dp, slice_rows, 3 * rank), F32),
-            pltpu.VMEM((dp, slice_rows, 3 * rank), F32),
-            pltpu.VMEM((seqs * half, 3 * rank), F32),
-            pltpu.VMEM((dp * tp, 8, LANES), F32),
+            pltpu.VMEM((dp, slice_rows, 3 * rank), BF16),
+            pltpu.VMEM((dp, slice_rows, 3 * rank), BF16),
+            pltpu.VMEM((dp, slice_rows, 3 * rank), BF16),
+            pltpu.VMEM((seqs * half, 3 * rank), BF16),
+            pltpu.VMEM((tp, 8, LANES), F32),
+            pltpu.VMEM((dp, 8, LANES), F32),
             dma((3, n_in)),
             dma((5,)),
             dma((CHUNKS, zs)),
@@ -459,14 +463,14 @@
             dma((CHUNKS, 2, 2 * zs)),
             dma((CHUNKS, dp)),
             dma((CHUNKS, dp)),
-            dma,
-            dma,
-            dma((dp,)),
-            dma((dp,)),
-            dma((dp,)),
-            dma((dp,)),
-            dma((dp * tp,)),
-            dma((dp * tp,)),
+            dma((2,)),
+            dma((2,)),
+            dma((dp,)),
+            dma((dp,)),
+            dma((dp,)),
+            dma((dp,)),
+            dma((dp,)),
+            dma((dp,)),
         ],
         compiler_params=pltpu.CompilerParams(
             collective_id=0, has_side_effects=True, vmem_limit_bytes=56 * 1024 * 1024

time: 54.8 us -> 50.4 us (0.920)
  Pallas kernels: 53.2 us -> 48.8 us
    pallas_call x1, Pallas kernels: 53.2 us -> 48.8 us  [local(): pl.pallas_call(functools.partial(kernel, (groups, dp, tp, rows, seqs, can...]
where the time goes in v3:
time: 50.4 us; the launch traced here: 50.1 us
  Pallas kernels  48.8 us (97%)
  local copies, waits for them, and re-layouts  1.32 us (3%)
    pallas_call x1, Pallas kernels, local(): pl.pallas_call(functools.partial(kernel, (groups, dp, tp, rows, seqs, can...  48.8 us
    unnamed x1, local copies, waits for them, and re-layouts  1.32 us

profile of v3, /device:TPU:0, one launch (start us, length us, event | category | flops | bytes accessed | tf_op | source)
XLA Modules:
  0.0 50.1 jit_solution(8254202145171349772)
XLA Ops:
  0.0 48.8 %shard_map.109 = f32[4,8,32]{2,1,0:T(8,128)} custom-call(s32[4]{0:T(128)} %len_ref.1, s32[4,8]{1,0:T(4,128)} %cand_ref.1, s32[4]{0:T(128)} %count_ref.1, bf16[96,4096]{1,0:T(8,128)(2,1)} %x_hbm.1, bf16[96,14336]{1,0:T(8,128)(2,1)} %gate_hbm.1, bf16[96,14336]{1,0:T(8,128)(2,1)} %up_hbm.1, bf16[96,14336]{1,0:T(8,128)(2,1)} %grad_hbm.1, ...), custom_call_target="tpu_custom_call" | custom-call | tf_op jit(solution)/shard_map/pallas_call | solution.py:432
  48.8 1.3 %copy.13 = f32[4,8,32]{2,1,0:T(8,128)} copy(f32[4,8,32]{2,1,0:T(8,128)} %shard_map.109) | data formatting | bytes 8192
